TPU v7x, 32 devices: a whole 2x2x4 slice. The times are simulated.
32 devices in a mesh: row: 4 (over y, core), col: 8 (over z, x).
Axes of the slice: x: 2, y: 2, z: 4, core: 2. Of those that a mesh axis runs over, the one named last changes fastest.
Arguments:
- points: float32 [4, 4, 256, 128], P(None, 'row'), may hold values from -1 to 1
- rhs: float32 [4, 4, 256, 256], P(None, 'row', None, 'col'), may hold values from -6 to 6
Outputs:
- factored: float32 [4, 4, 256, 2, 8, 256], P(None, 'row', None, None, 'col')
- solved: float32 [4, 4, 256, 256], P(None, 'row', None, 'col')
All inputs are finite; a program needn't handle non-finite values.
Results may differ from a plain program's by a relative error of at most 0.0003.
Values sent between devices are 32-bit elements; how exact they have to be, the bound alone decides.
A program may use at most 64 MiB of HBM per device.

v0:
```python
import jax
import jax.numpy as jnp
from jax import lax
from jax.sharding import PartitionSpec as P

PANELS = 2
SCALE = 3.0
NUGGET = 1.0
HIGHEST = lax.Precision.HIGHEST


def from_root(block, axis, owner):
    block = jnp.where(lax.axis_index(axis) == owner, block, jnp.zeros_like(block))
    return lax.psum(block, axis)


def kernel_tiles(left_points, right_points, left_index, right_index):
    feature_dim = left_points.shape[-1]
    left_sq = jnp.sum(left_points * left_points, axis=-1)
    right_sq = jnp.sum(right_points * right_points, axis=-1)
    inner_prod = jnp.einsum("ipf,jqf->ipjq", left_points, right_points, precision=HIGHEST)
    distance = left_sq[:, :, None, None] + right_sq[None, None, :, :] - 2.0 * inner_prod
    diagonal_hit = (left_index[:, :, None, None] == right_index[None, None, :, :]).astype(
        jnp.float32
    )
    return jnp.exp(-SCALE / feature_dim * distance) + NUGGET * diagonal_hit


def advance(current, panel_tiles, inverse, pivot_rhs, tile_of_row, which_panel):
    answer = jnp.dot(inverse, pivot_rhs, precision=HIGHEST)
    change = jnp.einsum("ipq,qn->ipn", panel_tiles, answer, precision=HIGHEST)
    below_rows = (tile_of_row > which_panel)[:, None, None]
    return (jnp.where(below_rows, current - change, current), answer)


def per_device(points, rhs):
    rows_n = lax.axis_size("row")
    cols_n = lax.axis_size("col")
    row_id = lax.axis_index("row")
    col_id = lax.axis_index("col")
    tile_rows = points.shape[0]
    tile_size = points.shape[2]
    feature_dim = points.shape[3]
    tile_cols = tile_rows * rows_n // cols_n
    stride = cols_n // rows_n
    row_points = points[:, 0]
    tile_of_row = jnp.arange(tile_rows, dtype=jnp.int32) * rows_n + row_id
    tile_of_col = jnp.arange(tile_cols, dtype=jnp.int32) * cols_n + col_id
    offsets = jnp.arange(tile_size, dtype=jnp.int32)
    row_index = tile_of_row[:, None] * tile_size + offsets[None, :]
    col_index = tile_of_col[:, None] * tile_size + offsets[None, :]
    grouped = row_points.reshape(tile_cols, stride, tile_size, feature_dim)
    chosen = lax.dynamic_index_in_dim(grouped, col_id // rows_n, 1, keepdims=False)
    col_points = from_root(chosen, "row", col_id % rows_n)
    kernel_grid = kernel_tiles(row_points, col_points, row_index, col_index)
    current = rhs[:, 0]
    identity = jnp.eye(tile_size, dtype=jnp.float32)
    row_panels = []
    answers = []
    for which_panel in range(PANELS):
        slot_a = which_panel // rows_n
        root_r = which_panel % rows_n
        slot_b = which_panel // cols_n
        root_c = which_panel % cols_n
        column_slab = kernel_grid[:, :, slot_b, :]
        pivot_tile, pivot_rhs = (
            from_root(column_slab[slot_a], "row", root_r),
            from_root(current[slot_a], "row", root_r),
        )
        factor = jnp.linalg.cholesky(pivot_tile)
        inverse = jax.scipy.linalg.solve_triangular(factor, identity, lower=True)
        panel_tiles = jnp.einsum("ipq,sq->ips", column_slab, inverse, precision=HIGHEST)
        panel_tiles, inverse = (
            from_root(panel_tiles, "col", root_c),
            from_root(inverse, "col", root_c),
        )
        grouped_panel = panel_tiles.reshape(tile_cols, stride, tile_size, tile_size)
        chosen_panel = lax.dynamic_index_in_dim(grouped_panel, col_id // rows_n, 1, keepdims=False)
        panel_cols = from_root(chosen_panel, "row", col_id % rows_n)
        kernel_grid = kernel_grid - jnp.einsum(
            "ipk,jqk->ipjq", panel_tiles, panel_cols, precision=HIGHEST
        )
        current, answer = advance(
            current, panel_tiles, inverse, pivot_rhs, tile_of_row, which_panel
        )
        row_panels.append(panel_tiles)
        answers.append(answer)
    solved = current
    for which_panel in range(PANELS):
        solved = jnp.where(
            (tile_of_row == which_panel)[:, None, None], answers[which_panel][None], solved
        )
    trailing_mask = (tile_of_row >= PANELS)[:, None, None, None] & (tile_of_col >= PANELS)[
        None, None, :, None
    ]
    factored = jnp.where(trailing_mask, kernel_grid, 0.0)
    beneath = row_index[:, :, None, None] >= col_index[None, None, :, :]
    for which_panel in range(PANELS):
        pick = beneath & (tile_of_col == which_panel)[None, None, :, None]
        factored = jnp.where(pick, row_panels[which_panel][:, :, None, :], factored)
    return (factored[:, None, :, :, None, :], solved[:, None])


def solution(mesh):
    return jax.shard_map(
        per_device,
        mesh=mesh,
        in_specs=(P(None, "row", None, None), P(None, "row", None, "col")),
        out_specs=(P(None, "row", None, None, "col", None), P(None, "row", None, "col")),
        check_vma=False,
    )
```

profile of v0, /device:TPU:0, one launch (start us, length us, event | category | flops | bytes accessed | tf_op | source)
XLA Modules:
  0.0 532.5 jit_solution(501918577944356869)
XLA Ops:
  7.2 1.7 fusion.18
  9.2 1.3 fusion.15
  10.4 35.2 %all-reduce.10.cloned.1.call-done = f32[2,256,128]{2,1,0:T(8,128)} async-done(((f32[2,256,128]{2,1,0:T(8,128)}), f32[2,256,128]{2,1,0:T(8,128)}) %all-reduce.10.cloned.1.call-update) | async-done | bytes 262160 | tf_op jit(solution)/shard_map/psum | solution.py:14
  45.6 1.1 multiply_reduce_fusion
  46.7 3.4 fusion.2
  51.4 31.7 %all-reduce.12.cloned.1.call-done = f32[256,256]{0,1:T(8,128)} async-done(((f32[256,256]{0,1:T(8,128)}), f32[256,256]{0,1:T(8,128)}) %all-reduce.12.cloned.1.call-update) | async-done | bytes 262160 | tf_op jit(solution)/shard_map/psum | solution.py:14
  83.1 1.1 copy.19
  84.2 1.0 fusion.22
  85.2 11.7 %cholesky.130 = f32[128,128]{1,0:T(8,128)S(1)} custom-call(f32[128,128]{1,0:T(8,128)S(1)} %cholesky.194), custom_call_target="Cholesky" | custom-call | tf_op jit(solution)/shard_map/jit(cholesky)/cholesky | solution.py:70
  96.9 9.8 %custom-call.13 = f32[1,128,128]{1,2,0:T(8,128)S(1)} custom-call(f32[1,128,128]{2,1,0:T(8,128)S(1)} %get-tuple-element.54), custom_call_target="InvertDiagBlocksLowerTriangular" | custom-call | tf_op jit(solution)/shard_map/jit(cholesky)/cholesky | solution.py:70
  107.3 11.7 %cholesky.147 = f32[128,128]{1,0:T(8,128)S(1)} custom-call(f32[128,128]{1,0:T(8,128)S(1)} %convolution_subtract_fusion.6), custom_call_target="Cholesky" | custom-call | tf_op jit(solution)/shard_map/jit(cholesky)/cholesky | solution.py:70
  121.1 4.6 while.4
  122.3 1.3 bitcast_dynamic-update-slice_fusion.4
  124.4 1.3 bitcast_dynamic-update-slice_fusion.4
  125.7 19.7 %custom-call.14 = f32[2,128,128]{1,2,0:T(8,128)S(1)} custom-call(f32[2,128,128]{2,1,0:T(8,128)S(1)} %get-tuple-element.18), custom_call_target="InvertDiagBlocksLowerTriangular" | custom-call | tf_op jit(solution)/shard_map/jit(_solve_triangular)/triangular_solve | solution.py:71
  146.3 2.9 convolution_select_fusion.1
  149.3 78.0 %all-reduce.14.cloned.1.call-done = f32[4,256,256]{2,1,0:T(8,128)} async-done(((f32[4,256,256]{2,1,0:T(8,128)}), f32[4,256,256]{2,1,0:T(8,128)}) %all-reduce.14.cloned.1.call-update) | async-done | bytes 1048592 | tf_op jit(solution)/shard_map/psum | solution.py:14
  227.3 2.0 fusion.11
  229.4 33.1 %all-reduce.16.cloned.1.call-done = f32[2,256,256]{2,1,0:T(8,128)} async-done(((f32[2,256,256]{2,1,0:T(8,128)}), f32[2,256,256]{2,1,0:T(8,128)}) %all-reduce.16.cloned.1.call-update) | async-done | bytes 524304 | tf_op jit(solution)/shard_map/psum | solution.py:14
  262.5 3.6 convolution_subtract_fusion
  267.1 1.6 fusion.26
  268.7 30.2 %all-reduce.18.cloned.1.call-done = f32[256,256]{0,1:T(8,128)} async-done(((f32[256,256]{0,1:T(8,128)}), f32[256,256]{0,1:T(8,128)}) %all-reduce.18.cloned.1.call-update) | async-done | bytes 262160 | tf_op jit(solution)/shard_map/psum | solution.py:14
  299.0 1.8 copy.23
  300.7 1.1 fusion.20
  302.5 11.7 %cholesky.164 = f32[128,128]{1,0:T(8,128)S(1)} custom-call(f32[128,128]{1,0:T(8,128)S(1)} %cholesky.197), custom_call_target="Cholesky" | custom-call | tf_op jit(solution)/shard_map/jit(cholesky)/cholesky | solution.py:70
  315.0 10.4 %custom-call.15 = f32[1,128,128]{1,2,0:T(8,128)} custom-call(f32[1,128,128]{2,1,0:T(8,128)S(1)} %get-tuple-element.50), custom_call_target="InvertDiagBlocksLowerTriangular" | custom-call | tf_op jit(solution)/shard_map/jit(cholesky)/cholesky | solution.py:70
  326.1 1.7 constant_dynamic-update-slice_fusion
  327.8 1.1 convolution_subtract_fusion.5
  328.9 11.7 %cholesky.181 = f32[128,128]{1,0:T(8,128)S(1)} custom-call(f32[128,128]{1,0:T(8,128)S(1)} %convolution_subtract_fusion.5), custom_call_target="Cholesky" | custom-call | tf_op jit(solution)/shard_map/jit(cholesky)/cholesky | solution.py:70
  344.0 5.9 %while.5 = (s32[]{:T(128)}, f32[256,256]{1,0:T(8,128)}, s32[2,2]{1,0:T(2,128)S(1)}, f32[2,128,128]{2,1,0:T(8,128)S(1)}, s32[]{:T(128)}) while((s32[]{:T(128)}, f32[256,256]{1,0:T(8,128)}, s32[2,2]{1,0:T(2,128)S(1)}, f32[2,128,128]{2,1,0:T(8,128)S(1)}, s32[]{:T(128)}) %tuple.73), condition=%wide.while_cond.clone, body=%wide.while_body.clone.sunk | while | flops 2 | bytes 131189 | solution.py:71
  344.8 2.3 bitcast_dynamic-update-slice_fusion.5
  347.7 2.2 bitcast_dynamic-update-slice_fusion.5
  350.5 20.5 %custom-call.16 = f32[2,128,128]{1,2,0:T(8,128)S(1)} custom-call(f32[2,128,128]{2,1,0:T(8,128)} %copy-done.6), custom_call_target="InvertDiagBlocksLowerTriangular" | custom-call | tf_op jit(solution)/shard_map/jit(_solve_triangular)/triangular_solve | solution.py:71
  371.3 1.1 convolution_subtract_fusion.3
  373.5 2.8 convolution_select_fusion
  376.4 10.7 %psum.86 = f32[256,32]{0,1:T(8,128)S(1)} all-reduce(f32[256,32]{0,1:T(8,128)S(1)} %select_bitcast_fusion.3), channel_id=1, replica_groups=mesh['row'=4,'col'=8] {'row'}, use_global_device_ids=true, to_apply=%region_15.18 | all-reduce | flops 8192 | bytes 65536 | tf_op jit(solution)/shard_map/psum | solution.py:14
  387.2 1.3 copy.26
  388.5 77.7 %all-reduce.22.cloned.1.call-done = (f32[4,256,256]{2,1,0:T(8,128)}, f32[256,256]{1,0:T(8,128)}, f32[256,256]{1,0:T(8,128)}) async-done(((f32[4,256,256]{2,1,0:T(8,128)}, f32[256,256]{1,0:T(8,128)}, f32[256,256]{1,0:T(8,128)}), (f32[4,256,256]{2,1,0:T(8,128)}, f32[256,256]{1,0:T(8,128)}, f32[256,256]{1,0:T(8,128)})) %all-reduce.22.cloned.1.call-update) | async-done | bytes 1572880 | tf_op jit(solution)/shard_map/psum | solution.py:14
  466.2 1.4 fusion.48
  467.6 2.3 fusion.4
  469.9 11.3 %psum.87 = f32[256,32]{0,1:T(8,128)S(1)} all-reduce(f32[256,32]{0,1:T(8,128)S(1)} %fusion.41), channel_id=1, replica_groups=mesh['row'=4,'col'=8] {'row'}, use_global_device_ids=true, to_apply=%region_16.19 | all-reduce | flops 8192 | bytes 65536 | tf_op jit(solution)/shard_map/psum | solution.py:14
  481.2 0.8 fusion.10
  482.1 1.3 fusion.49
  483.4 1.3 copy.25
  484.7 1.7 fusion.7
  486.4 27.5 %all-reduce.20.cloned.1.call-done = f32[2,256,256]{2,1,0:T(8,128)} async-done(((f32[2,256,256]{2,1,0:T(8,128)}), f32[2,256,256]{2,1,0:T(8,128)}) %all-reduce.20.cloned.1.call-update) | async-done | bytes 524304 | tf_op jit(solution)/shard_map/psum | solution.py:14
  513.9 5.5 %select_bitcast_fusion = f32[4,1,256,2,1,256]{2,5,3,0,4,1:T(8,128)} fusion(f32[4,256,2,256]{1,3,2,0:T(8,128)S(1)} %convolution_subtract_fusion, f32[4,256,256]{2,1,0:T(8,128)S(1)} %copy-done, f32[4,256,256]{1,2,0:T(8,128)} %copy.26, f32[4,256,256]{1,2,0:T(8,128)} %copy.25, s32[2,256]{1,0:T(2,128)S(1)} %iota_add_fusion.1, s32[4,256]{1,0:T(4,128)S(1)} %iota_add_fusion, ...), kind=kOutput, calls=%fused_computation.10 | convolution fusion | flops 1614282752 | bytes 7870476 | tf_op jit(solution)/shard_map/ipk,jqk->ipjq/dot_general | solution.py:80
  519.4 6.0 %copy.29 = f32[4,1,256,2,1,256]{5,4,3,2,1,0:T(1,128)} copy(f32[4,1,256,2,1,256]{2,5,3,0,4,1:T(8,128)} %select_bitcast_fusion) | data formatting | bytes 4194304
  (76 shorter events, 13.7 us)
Async XLA Ops:
  7.2 38.4 %all-reduce.10.cloned.1.call-start = ((), (), s32[]{:S(2)}) async-start(), calls=%async_computation | async-start | bytes 524288 | tf_op jit(solution)/shard_map/psum | solution.py:14
  8.9 74.2 %all-reduce.12.cloned.1.call-start = ((), (), s32[]{:S(2)}) async-start(), calls=%async_computation.1 | async-start | bytes 524288 | tf_op jit(solution)/shard_map/psum | solution.py:14
  50.2 96.1 %copy-start.2 = (f32[4,256,2,256]{1,3,2,0:T(8,128)}, f32[4,256,2,256]{1,3,2,0:T(8,128)S(1)}, u32[]{:S(2)}) copy-start(f32[4,256,2,256]{1,3,2,0:T(8,128)S(1)} %fusion.2) | copy-start | bytes 6291460
  51.0 176.3 %all-reduce.14.cloned.1.call-start = ((), (), s32[]{:S(2)}) async-start(), calls=%async_computation.2 | async-start | bytes 2097152 | tf_op jit(solution)/shard_map/psum | solution.py:14
  146.3 2.9 copy-start.3
  149.2 113.3 %all-reduce.16.cloned.1.call-start = ((), (), s32[]{:S(2)}) async-start(), calls=%async_computation.3 | async-start | bytes 1048576 | tf_op jit(solution)/shard_map/psum | solution.py:14
  227.3 35.2 %copy-start.1 = (f32[4,256,256]{2,1,0:T(8,128)S(1)}, f32[4,256,256]{2,1,0:T(8,128)}, u32[]{:S(2)}) copy-start(f32[4,256,256]{2,1,0:T(8,128)} %all-reduce.14.cloned.1.call-done) | copy-start | bytes 3145732
  229.3 69.7 %all-reduce.18.cloned.1.call-start = ((), (), s32[]{:S(2)}) async-start(), calls=%async_computation.4 | async-start | bytes 524288 | tf_op jit(solution)/shard_map/psum | solution.py:14
  266.8 199.3 %all-reduce.22.cloned.1.call-start = ((), (), s32[]{:S(2)}) async-start(), calls=%async_computation.6 | async-start | bytes 3145728 | tf_op jit(solution)/shard_map/psum | solution.py:14
  301.8 0.7 copy-start.4
  349.9 0.7 copy-start.6
  373.5 2.9 copy-start.5
  376.3 137.7 %all-reduce.20.cloned.1.call-start = ((), (), s32[]{:S(2)}) async-start(), calls=%async_computation.5 | async-start | bytes 1048576 | tf_op jit(solution)/shard_map/psum | solution.py:14
  466.2 15.0 %copy-start = (f32[4,256,256]{2,1,0:T(8,128)S(1)}, f32[4,256,256]{2,1,0:T(8,128)}, u32[]{:S(2)}) copy-start(f32[4,256,256]{2,1,0:T(8,128)} %get-tuple-element.40) | copy-start | bytes 3145732
Sparse Core Ops, SparseCore 0:
  10.9 34.6 all-reduce.9
  51.1 31.9 all-reduce.11
  149.3 77.9 all-reduce.13
  229.6 32.7 all-reduce.15
  267.0 31.9 all-reduce.17
  376.4 89.7 all-reduce.21
  482.2 31.6 all-reduce.19
where the time goes:
time: 536 us; the launch traced here: 533 us
  waiting for transfers between devices  314 us (59%)
  other arithmetic  124 us (23%)
  matrix products  30.8 us (6%)
  local copies, waits for them, and re-layouts  23.4 us (4%)
  blocking collectives  22 us (4%)
  between operations  17.3 us (3%)
    psum x7, waiting for transfers between devices, from_root(): return lax.psum(block, axis)  313 us
    another operation x13, other arithmetic, per_device(): factor = jnp.linalg.cholesky(pivot_tile)  69.9 us
    another operation x5, other arithmetic, per_device(): inverse = jax.scipy.linalg.solve_triangular(factor, identity, lower=True)  40.9 us
    psum x2, blocking collectives, from_root(): return lax.psum(block, axis)  22 us
  transfers between devices with their start and end apart: 7, of which 7 were waited for; matrix products, arithmetic and copies ran while one was open for 2% of the time, Pallas kernels for 0%

commit v1 on v0

--- a/solution.py
+++ b/solution.py
@@ -9,9 +9,15 @@
 HIGHEST = lax.Precision.HIGHEST
 
 
+def add_all(x, mesh_axis):
+    shards = lax.all_gather(x, mesh_axis, axis=0, tiled=False)
+    summed = shards.sum(axis=0)
+    return summed
+
+
 def from_root(block, axis, owner):
     block = jnp.where(lax.axis_index(axis) == owner, block, jnp.zeros_like(block))
-    return lax.psum(block, axis)
+    return add_all(block, axis)
 
 
 def kernel_tiles(left_points, right_points, left_index, right_index):

time: 536 us -> 652 us (1.22)
  waiting for transfers between devices: 314 us -> 419 us
  other arithmetic: 124 us -> 145 us
  blocking collectives: 22 us -> 10.9 us
    all_gather x0 -> x9, waiting for transfers between devices: none -> 419 us  [add_all(): shards = lax.all_gather(x, mesh_axis, axis=0, tiled=False)]
    psum x7 -> x0, waiting for transfers between devices: 313 us -> none  [from_root(): return lax.psum(block, axis)]
    psum x2 -> x0, blocking collectives: 22 us -> none  [from_root(): return lax.psum(block, axis)]
    reduce_sum x0 -> x11, other arithmetic: none -> 19.2 us  [add_all(): summed = shards.sum(axis=0)]
    all_gather x0 -> x2, blocking collectives: none -> 10.9 us  [add_all(): shards = lax.all_gather(x, mesh_axis, axis=0, tiled=False)]
  transfers between devices with their start and end apart: 7 -> 9, of which waited for: 7 -> 9; matrix products, arithmetic and copies ran while one was open for 2% -> 3% of each run, Pallas kernels for 0% -> 0%
where the time goes in v1:
time: 652 us; the launch traced here: 648 us
  waiting for transfers between devices  419 us (64%)
  other arithmetic  145 us (22%)
  matrix products  28.7 us (4%)
  local copies, waits for them, and re-layouts  24.6 us (4%)
  between operations  17.2 us (3%)
  blocking collectives  10.9 us (2%)
    all_gather x9, waiting for transfers between devices, add_all(): shards = lax.all_gather(x, mesh_axis, axis=0, tiled=False)  419 us
    another operation x13, other arithmetic, per_device(): factor = jnp.linalg.cholesky(pivot_tile)  76 us
    another operation x5, other arithmetic, per_device(): inverse = jax.scipy.linalg.solve_triangular(factor, identity, lower=True)  41.5 us
    reduce_sum x11, other arithmetic, add_all(): summed = shards.sum(axis=0)  19.2 us
  transfers between devices with their start and end apart: 9, of which 9 were waited for; matrix products, arithmetic and copies ran while one was open for 3% of the time, Pallas kernels for 0%

profile of v1, /device:TPU:0, one launch (start us, length us, event | category | flops | bytes accessed | tf_op | source)
XLA Modules:
  0.0 647.6 jit_solution(3749464608499495141)
XLA Ops:
  7.3 1.7 dynamic-slice_select_fusion.2
  10.5 19.1 %all-gather.20.cloned.1.call-done = f32[8,1,256,128]{3,2,1,0:T(8,128)} async-done(((f32[2,1,256,128]{3,2,1,0:T(8,128)}), f32[8,1,256,128]{3,2,1,0:T(8,128)}) %all-gather.20.cloned.1.call-update) | async-done | bytes 1048592 | tf_op jit(solution)/shard_map/all_gather | solution.py:13
  29.6 1.3 bitcast_reduce_fusion.2
  31.1 2.3 fusion.2
  34.9 16.5 %all-gather.22.cloned.1.call-done = f32[4,256,1,256]{3,1,2,0:T(8,128)} async-done(((f32[1,256,1,256]{3,1,2,0:T(8,128)}), f32[4,256,1,256]{3,1,2,0:T(8,128)}) %all-gather.22.cloned.1.call-update) | async-done | bytes 1048592 | tf_op jit(solution)/shard_map/all_gather | solution.py:13
  51.4 1.3 reduce_sum.120
  52.9 11.7 %cholesky.130 = f32[128,128]{1,0:T(8,128)S(1)} custom-call(f32[128,128]{1,0:T(8,128)S(1)} %cholesky.194), custom_call_target="Cholesky" | custom-call | tf_op jit(solution)/shard_map/jit(cholesky)/cholesky | solution.py:76
  64.7 9.8 %custom-call.13 = f32[1,128,128]{1,2,0:T(8,128)S(1)} custom-call(f32[1,128,128]{2,1,0:T(8,128)S(1)} %get-tuple-element.53), custom_call_target="InvertDiagBlocksLowerTriangular" | custom-call | tf_op jit(solution)/shard_map/jit(cholesky)/cholesky | solution.py:76
  75.0 11.7 %cholesky.147 = f32[128,128]{1,0:T(8,128)S(1)} custom-call(f32[128,128]{1,0:T(8,128)S(1)} %convolution_subtract_fusion.6), custom_call_target="Cholesky" | custom-call | tf_op jit(solution)/shard_map/jit(cholesky)/cholesky | solution.py:76
  88.9 4.7 while.4
  90.1 1.4 bitcast_dynamic-update-slice_fusion.4
  92.2 1.4 bitcast_dynamic-update-slice_fusion.4
  93.6 19.7 %custom-call.14 = f32[2,128,128]{1,2,0:T(8,128)S(1)} custom-call(f32[2,128,128]{2,1,0:T(8,128)S(1)} %get-tuple-element.18), custom_call_target="InvertDiagBlocksLowerTriangular" | custom-call | tf_op jit(solution)/shard_map/jit(_solve_triangular)/triangular_solve | solution.py:77
  114.2 2.9 convolution_select_fusion.1
  117.2 125.0 %all-gather.24.cloned.1.call-done = f32[32,256,256]{2,1,0:T(8,128)} async-done(((f32[4,256,256]{2,1,0:T(8,128)}), f32[32,256,256]{2,1,0:T(8,128)}) %all-gather.24.cloned.1.call-update) | async-done | bytes 8388624 | tf_op jit(solution)/shard_map/all_gather | solution.py:13
  242.2 4.1 reduce_sum.121
  247.2 20.9 %all-gather.26.cloned.1.call-done = f32[8,1,256,256]{3,2,1,0:T(8,128)} async-done(((f32[2,1,256,256]{3,2,1,0:T(8,128)}), f32[8,1,256,256]{3,2,1,0:T(8,128)}) %all-gather.26.cloned.1.call-update) | async-done | bytes 2097168 | tf_op jit(solution)/shard_map/all_gather | solution.py:13
  268.1 1.8 bitcast_reduce_fusion.1
  269.9 3.5 convolution_subtract_fusion
  274.7 16.7 %all-gather.28.cloned.1.call-done = f32[4,256,1,256]{3,1,2,0:T(8,128)} async-done(((f32[1,256,1,256]{3,1,2,0:T(8,128)}), f32[4,256,1,256]{3,1,2,0:T(8,128)}) %all-gather.28.cloned.1.call-update) | async-done | bytes 1048592 | tf_op jit(solution)/shard_map/all_gather | solution.py:13
  291.3 1.3 reduce_sum.123
  295.8 13.2 %cholesky.164 = f32[128,128]{1,0:T(8,128)} custom-call(f32[128,128]{1,0:T(8,128)} %cholesky.197), custom_call_target="Cholesky" | custom-call | tf_op jit(solution)/shard_map/jit(cholesky)/cholesky | solution.py:76
  309.0 1.5 select_reduce_fusion.1
  310.5 1.6 cholesky.189
  312.0 11.3 %custom-call.15 = f32[1,128,128]{1,2,0:T(8,128)} custom-call(f32[1,128,128]{2,1,0:T(8,128)} %get-tuple-element.49), custom_call_target="InvertDiagBlocksLowerTriangular" | custom-call | tf_op jit(solution)/shard_map/jit(cholesky)/cholesky | solution.py:76
  323.3 1.7 constant_dynamic-update-slice_fusion
  325.0 1.7 convolution_subtract_fusion.5
  326.7 13.2 %cholesky.181 = f32[128,128]{1,0:T(8,128)} custom-call(f32[128,128]{1,0:T(8,128)} %convolution_subtract_fusion.5), custom_call_target="Cholesky" | custom-call | tf_op jit(solution)/shard_map/jit(cholesky)/cholesky | solution.py:76
  339.9 1.5 select_reduce_fusion
  345.5 7.2 %while.5 = (s32[]{:T(128)}, f32[256,256]{1,0:T(8,128)}, s32[2,2]{1,0:T(2,128)S(1)}, f32[2,128,128]{2,1,0:T(8,128)}, s32[]{:T(128)}) while((s32[]{:T(128)}, f32[256,256]{1,0:T(8,128)}, s32[2,2]{1,0:T(2,128)S(1)}, f32[2,128,128]{2,1,0:T(8,128)}, s32[]{:T(128)}) %tuple.76), condition=%wide.while_cond.clone, body=%wide.while_body.clone.sunk | while | flops 2 | bytes 132705 | solution.py:77
  346.3 2.9 bitcast_dynamic-update-slice_fusion.5
  349.9 2.8 bitcast_dynamic-update-slice_fusion.5
  352.7 21.1 %custom-call.16 = f32[2,128,128]{1,2,0:T(8,128)} custom-call(f32[2,128,128]{2,1,0:T(8,128)} %get-tuple-element.19), custom_call_target="InvertDiagBlocksLowerTriangular" | custom-call | tf_op jit(solution)/shard_map/jit(_solve_triangular)/triangular_solve | solution.py:77
  377.3 2.9 convolution_select_fusion
  381.1 1.6 fusion.20
  382.8 122.5 %all-gather.30.cloned.1.call-done = f32[32,256,256]{2,1,0:T(8,128)} async-done(((f32[4,256,256]{2,1,0:T(8,128)}), f32[32,256,256]{2,1,0:T(8,128)}) %all-gather.30.cloned.1.call-update) | async-done | bytes 8388624 | tf_op jit(solution)/shard_map/all_gather | solution.py:13
  505.3 4.1 reduce_sum.124
  510.3 5.4 all-gather.9
  515.9 39.1 %all-gather.36.cloned.1.call-done = f32[2048,256]{1,0:T(8,128)} async-done(((f32[256,256]{1,0:T(8,128)}), f32[2048,256]{1,0:T(8,128)}) %all-gather.36.cloned.1.call-update) | async-done | bytes 2097168 | tf_op jit(solution)/shard_map/all_gather | solution.py:13
  554.9 1.8 reduce_sum.127
  558.5 5.4 all_gather.66
  563.9 41.0 %all-gather.34.cloned.1.call-done = f32[2048,256]{1,0:T(8,128)} async-done(((f32[256,256]{1,0:T(8,128)}), f32[2048,256]{1,0:T(8,128)}) %all-gather.34.cloned.1.call-update) | async-done | bytes 2097168 | tf_op jit(solution)/shard_map/all_gather | solution.py:13
  604.9 1.8 reduce_sum.126
  607.3 1.7 fusion.7
  609.0 18.5 %all-gather.32.cloned.1.call-done = f32[8,1,256,256]{3,2,1,0:T(8,128)} async-done(((f32[2,1,256,256]{3,2,1,0:T(8,128)}), f32[8,1,256,256]{3,2,1,0:T(8,128)}) %all-gather.32.cloned.1.call-update) | async-done | bytes 2097168 | tf_op jit(solution)/shard_map/all_gather | solution.py:13
  627.5 1.8 bitcast_reduce_fusion
  629.3 5.4 select_bitcast_fusion
  634.8 6.1 copy.36
  (102 shorter events, 24.1 us)
Async XLA Ops:
  7.2 23.9 %copy-start.7 = (f32[4,1,256,128]{3,2,1,0:T(8,128)S(1)}, f32[4,1,256,128]{3,2,1,0:T(8,128)}, u32[]{:S(2)}) copy-start(f32[4,1,256,128]{3,2,1,0:T(8,128)} %param.5) | copy-start | bytes 1572868
  7.2 22.4 %all-gather.20.cloned.1.call-start = ((), (), s32[]{:S(2)}) async-start(), calls=%async_computation | async-start | bytes 1310720 | tf_op jit(solution)/shard_map/all_gather | solution.py:13
  9.0 42.4 %all-gather.22.cloned.1.call-start = ((), (), s32[]{:S(2)}) async-start(), calls=%async_computation.1 | async-start | bytes 1310720 | tf_op jit(solution)/shard_map/all_gather | solution.py:13
  33.4 80.8 %copy-start.1 = (f32[4,256,2,256]{1,3,0,2:T(8,128)}, f32[4,256,2,256]{1,3,0,2:T(8,128)S(1)}, u32[]{:S(2)}) copy-start(f32[4,256,2,256]{1,3,0,2:T(8,128)S(1)} %fusion.2) | copy-start | bytes 6291460
  34.5 207.7 %all-gather.24.cloned.1.call-start = ((), (), s32[]{:S(2)}) async-start(), calls=%async_computation.2 | async-start | bytes 9437184 | tf_op jit(solution)/shard_map/all_gather | solution.py:13
  34.9 78.7 %copy-start.2 = (f32[256,256]{1,0:T(8,128)}, f32[256,256]{1,0:T(8,128)S(1)}, u32[]{:S(2)}) copy-start(f32[256,256]{1,0:T(8,128)S(1)} %fusion.19) | copy-start | bytes 786436
  114.2 132.1 %copy-start.5 = (f32[128,256]{1,0:T(8,128)}, f32[128,256]{1,0:T(8,128)S(1)}, u32[]{:S(2)}) copy-start(f32[128,256]{1,0:T(8,128)S(1)} %fusion.31) | copy-start | bytes 393220
  117.1 151.0 %all-gather.26.cloned.1.call-start = ((), (), s32[]{:S(2)}) async-start(), calls=%async_computation.3 | async-start | bytes 2621440 | tf_op jit(solution)/shard_map/all_gather | solution.py:13
  247.1 44.2 %all-gather.28.cloned.1.call-start = ((), (), s32[]{:S(2)}) async-start(), calls=%async_computation.4 | async-start | bytes 1310720 | tf_op jit(solution)/shard_map/all_gather | solution.py:13
  273.4 109.3 %copy-start = (f32[4,256,2,256]{1,3,0,2:T(8,128)}, f32[4,256,2,256]{1,3,0,2:T(8,128)S(1)}, u32[]{:S(2)}) copy-start(f32[4,256,2,256]{1,3,0,2:T(8,128)S(1)} %convolution_subtract_fusion) | copy-start | bytes 6291460
  274.4 230.8 %all-gather.30.cloned.1.call-start = ((), (), s32[]{:S(2)}) async-start(), calls=%async_computation.5 | async-start | bytes 9437184 | tf_op jit(solution)/shard_map/all_gather | solution.py:13
  294.5 0.7 copy-start.8
  295.2 78.6 %copy-start.3 = (f32[256,256]{1,0:T(8,128)S(1)}, f32[256,256]{1,0:T(8,128)}, u32[]{:S(2)}) copy-start(f32[256,256]{1,0:T(8,128)} %copy-done.2) | copy-start | bytes 786436
  374.9 2.4 copy-start.4
  376.1 4.2 copy-start.6
  380.2 174.7 %all-gather.36.cloned.1.call-start = ((), (), s32[]{:S(2)}) async-start(), calls=%async_computation.8 | async-start | bytes 2359296 | tf_op jit(solution)/shard_map/all_gather | solution.py:13
  381.0 223.9 %all-gather.34.cloned.1.call-start = ((), (), s32[]{:S(2)}) async-start(), calls=%async_computation.7 | async-start | bytes 2359296 | tf_op jit(solution)/shard_map/all_gather | solution.py:13
  382.7 244.8 %all-gather.32.cloned.1.call-start = ((), (), s32[]{:S(2)}) async-start(), calls=%async_computation.6 | async-start | bytes 2621440 | tf_op jit(solution)/shard_map/all_gather | solution.py:13
  505.3 4.9 copy-start.9
Sparse Core Ops, SparseCore 0:
  10.1 19.4 all-gather.19
  34.6 16.7 all-gather.21
  117.2 124.9 all-gather.23
  247.3 20.7 all-gather.25
  274.6 16.7 all-gather.27
  380.3 124.9 all-gather.29
  507.4 47.4 all-gather.35
  557.0 47.7 all-gather.33
  606.4 21.0 all-gather.31
